TPU v7x, 32 devices: a whole 2x2x4 slice. The times are simulated.
32 devices in a mesh: dom: 2 (over x), wide: 8 (over z, y), grad: 2 (over core).
Axes of the slice: x: 2, y: 2, z: 4, core: 2. Of those that a mesh axis runs over, the one named last changes fastest.
Arguments:
- activations: bfloat16 [16, 2048, 2048], P(('dom', 'wide'), 'grad'), parts along dimension 0, may hold values from -3 to 3
- inverse: bfloat16 [16, 2048, 2048], P(('dom', 'wide'), 'grad'), parts along dimension 0, as said below
- gradients: bfloat16 [16, 2048, 384], P(('dom', 'wide'), 'grad'), parts along dimension 0, may hold values from -6 to 6
- matching: int32 [16], P('dom'), parts along dimension 0, may hold values from 0 to 7, each once
- live_rows: int32 [16], P('dom'), parts along dimension 0, may hold values from 1 to 2048, 12288 in all
Outputs:
- preconditioned: bfloat16 [16, 2048, 384], P(('dom', 'wide'), 'grad'), parts along dimension 0
There are 2 independent parts, one for each index of `dom`. A program takes and returns all parts, laid end to end along the dimension named above; each array names one. Nothing has to cross between parts.
Inputs may be any that keep to these rules, and one draw needn't show every extreme that they name: matching names every index of wide once; inverse tile s is used for the tile of index matching[s]. The live rows of tile t are its first live_rows[t] rows; some tile has all 2048. `inverse`: symmetric.
All inputs are finite; a program needn't handle non-finite values.
Results may differ from a plain program's by a relative error of at most 0.0059.
Values may be sent and summed in bfloat16 or wider, within the bound.
A program may use at most 128 MiB of HBM per device.

v0:
```python
import jax
import jax.numpy as jnp
from jax import lax
from jax.sharding import PartitionSpec as P

DAMPING = 1.0


def regroup(stacked, destination, groups):
    grouped = stacked.reshape((groups, stacked.shape[0] // groups) + stacked.shape[1:])
    return jnp.take(grouped, destination, axis=0).reshape(stacked.shape)


def product_step(matrix, shard_rows):
    return jnp.dot(matrix, shard_rows, preferred_element_type=jnp.float32)


def build_factor(tile_rows, row_count):
    core_index = lax.axis_index("grad")
    tile_order = tile_rows.shape[1]
    half_rows = tile_order // lax.axis_size("grad")
    live_count = row_count.astype(jnp.float32)
    shard_rows = lax.all_gather(tile_rows, "grad", axis=0, tiled=True)
    keep_rows = jnp.arange(shard_rows.shape[0], dtype=jnp.int32) < row_count
    masked = jnp.where(keep_rows[:, None], shard_rows, jnp.zeros_like(shard_rows))
    columns = lax.dynamic_slice_in_dim(shard_rows, core_index * half_rows, half_rows, 1)
    factor = jnp.einsum("rh,rc->hc", columns, masked, preferred_element_type=jnp.float32)
    diagonal = (core_index * half_rows + jnp.arange(half_rows, dtype=jnp.int32))[
        :, None
    ] == jnp.arange(tile_order, dtype=jnp.int32)[None, :]
    return (factor / live_count + jnp.where(diagonal, DAMPING, 0.0)).astype(jnp.bfloat16)


def first_product(inverse_rows, grad_rows):
    return product_step(inverse_rows, lax.all_gather(grad_rows, "grad", axis=0, tiled=True))


def curvature_product(damped, first_round):
    return product_step(damped, lax.all_gather(first_round, "grad", axis=0, tiled=True)).astype(
        jnp.bfloat16
    )


def correction_product(inverse_rows, curvature):
    return product_step(inverse_rows, lax.all_gather(curvature, "grad", axis=0, tiled=True))


def precondition(inverse_rows, tile_rows, grad_rows, row_count):
    damped = build_factor(tile_rows, row_count)
    first_sum = first_product(inverse_rows, grad_rows)
    curvature = curvature_product(damped, first_sum.astype(jnp.bfloat16))
    correction = correction_product(inverse_rows, curvature)
    return (2.0 * first_sum - correction).astype(jnp.bfloat16)


def per_device(activations, inverse, gradients, matching, live_rows):
    wide_size = lax.axis_size("wide")
    position = lax.axis_index("wide")
    places = jnp.arange(wide_size, dtype=jnp.int32)
    sources = jnp.sum(jnp.where(matching[None, :] == places[:, None], places[None, :], 0), axis=1)
    spread = lax.all_to_all(inverse[0], "wide", split_axis=0, concat_axis=0, tiled=True)
    settled = lax.all_to_all(
        regroup(spread, sources, wide_size), "wide", split_axis=0, concat_axis=0, tiled=True
    )
    result = precondition(settled, activations[0], gradients[0], live_rows[position])
    return result[None]


def solution(mesh):
    return jax.shard_map(
        per_device,
        mesh=mesh,
        in_specs=(
            P(("dom", "wide"), "grad", None),
            P(("dom", "wide"), "grad", None),
            P(("dom", "wide"), "grad", None),
            P("dom"),
            P("dom"),
        ),
        out_specs=P(("dom", "wide"), "grad", None),
        check_vma=False,
    )
```

profile of v0, /device:TPU:0, one launch (start us, length us, event | category | flops | bytes accessed | tf_op | source)
XLA Modules:
  0.0 263.2 jit_solution(1911316350643083428)
XLA Ops:
  6.5 7.3 %all-to-all-start = ((bf16[8,128,2048]{2,1,0:T(8,128)(2,1)}), bf16[8,128,2048]{2,1,0:T(8,128)(2,1)}, u32[]{:S(2)}, u32[]{:S(2)}) async-start(bf16[8,128,2048]{2,1,0:T(8,128)(2,1)} %bitcast.24), calls=%async_computation | async-start | bytes 8388608 | tf_op jit(solution)/shard_map/all_to_all | solution.py:61
  13.8 0.0 copy-start
  13.8 0.0 all-gather.11.cloned.1.call-start
  13.9 0.7 all-gather.11.cloned.1.call-update
  14.6 0.0 all-gather.13.cloned.1.call-start
  14.6 0.7 all-gather.13.cloned.1.call-update
  15.3 0.0 copy-done
  15.3 0.1 select_reduce_fusion
  15.5 91.6 %all-to-all-done = bf16[8,128,2048]{2,1,0:T(8,128)(2,1)} async-done(((bf16[8,128,2048]{2,1,0:T(8,128)(2,1)}), bf16[8,128,2048]{2,1,0:T(8,128)(2,1)}, u32[]{:S(2)}, u32[]{:S(2)}) %all-to-all-start) | async-done | bytes 4194336 | tf_op jit(solution)/shard_map/all_to_all | solution.py:61
  107.1 4.9 %gather_fusion = bf16[8,128,2048]{2,1,0:T(8,128)(2,1)} fusion(bf16[8,128,2048]{2,1,0:T(8,128)(2,1)} %all-to-all-done, s32[1024]{0:T(1024)S(1)} %pad_clamp_fusion), kind=kCustom, calls=%fused_computation | custom fusion | bytes 8388640 | tf_op jit(solution)/shard_map/jit(_take)/gather | solution.py:11
  112.0 4.6 %broadcast_select_fusion = bf16[8,128,2048]{2,1,0:T(8,128)(2,1)} fusion(bf16[8,128,2048]{2,1,0:T(8,128)(2,1)} %gather_fusion, pred[8]{0:T(512)(128)(4,1)S(1)} %compare_and_fusion), kind=kLoop, calls=%fused_computation.9 | loop fusion | flops 2097152 | bytes 8388616 | tf_op jit(solution)/shard_map/jit(_take)/select_n | solution.py:11
  116.6 0.0 copy-start.1
  116.6 4.7 %all-to-all-start.1 = ((bf16[8,128,2048]{2,1,0:T(8,128)(2,1)}), bf16[8,128,2048]{2,1,0:T(8,128)(2,1)}, u32[]{:S(2)}, u32[]{:S(2)}) async-start(bf16[8,128,2048]{2,1,0:T(8,128)(2,1)} %broadcast_select_fusion), calls=%async_computation.1 | async-start | bytes 8388608 | tf_op jit(solution)/shard_map/all_to_all | solution.py:62
  121.3 0.0 all-gather.7.cloned.1.call-start
  121.4 0.0 copy-done.1
  121.4 0.6 dynamic_slice.7
  122.6 0.7 iota_compare_fusion.1
  123.3 0.0 all-gather.11.cloned.1.call-done
  123.3 90.5 %all-to-all-done.1 = bf16[8,128,2048]{2,1,0:T(8,128)(2,1)} async-done(((bf16[8,128,2048]{2,1,0:T(8,128)(2,1)}), bf16[8,128,2048]{2,1,0:T(8,128)(2,1)}, u32[]{:S(2)}, u32[]{:S(2)}) %all-to-all-start.1) | async-done | bytes 4194336 | tf_op jit(solution)/shard_map/all_to_all | solution.py:62
  213.9 5.9 %fusion.15 = (bf16[1024,384]{1,0:T(8,128)(2,1)}, f32[1024,384]{1,0:T(8,128)S(1)}) fusion(bf16[1024,2048]{1,0:T(8,128)(2,1)} %bitcast.3, bf16[1,2048,384]{2,1,0:T(8,128)(2,1)} %all-gather.11.cloned.1.call-done), kind=kOutput, calls=%fused_computation.29 | convolution fusion | flops 1611005952 | bytes 8126464 | tf_op jit(solution)/shard_map/dot_general | solution.py:15
  219.7 0.0 all-gather.7.cloned.1.call-update
  219.8 0.0 all-gather.9.cloned.1.call-start
  219.8 0.0 all-gather.13.cloned.1.call-done
  219.8 14.8 %fusion = f32[1024,2048]{1,0:T(8,128)} fusion(bf16[1,2048,2048]{2,1,0:T(8,128)(2,1)} %all-gather.13.cloned.1.call-done, pred[2048]{0:T(1024)(128)(4,1)S(1)} %iota_compare_fusion.1, s32[]{:T(128)S(6)} %select_n.44), kind=kOutput, calls=%fused_computation.2 | convolution fusion | flops 8594128896 | bytes 20973572 | tf_op jit(solution)/shard_map/rh,rc->hc/dot_general | solution.py:27
  234.7 0.0 all-gather.7.cloned.1.call-done
  234.7 7.1 %fusion.8 = bf16[1024,384]{1,0:T(8,128)(2,1)} fusion(bf16[2048,384]{1,0:T(8,128)(2,1)} %all-gather.7.cloned.1.call-done, f32[1024,2048]{1,0:T(8,128)} %fusion, s32[1024]{0:T(1024)S(1)} %iota_add_fusion, f32[]{:T(128)S(6)} %convert_element_type.15), kind=kOutput, calls=%fused_computation.14 | convolution fusion | flops 1621491712 | bytes 10752004 | tf_op jit(solution)/shard_map/dot_general | solution.py:15
  241.7 0.0 all-gather.9.cloned.1.call-update
  241.8 9.0 %all-gather.9.cloned.1.call-done = bf16[2048,384]{1,0:T(8,128)(2,1)} async-done(((bf16[1024,384]{1,0:T(8,128)(2,1)}), bf16[2048,384]{1,0:T(8,128)(2,1)}) %all-gather.9.cloned.1.call-update) | async-done | bytes 1572880 | tf_op jit(solution)/shard_map/all_gather | solution.py:45
  250.8 5.9 %fusion.9 = bf16[1,1024,384]{2,1,0:T(8,128)(2,1)} fusion(bf16[1024,2048]{1,0:T(8,128)(2,1)} %bitcast.3, bf16[2048,384]{1,0:T(8,128)(2,1)} %all-gather.9.cloned.1.call-done, f32[1024,384]{1,0:T(8,128)S(1)} %get-tuple-element.6), kind=kOutput, calls=%fused_computation.15 | convolution fusion | flops 1611792384 | bytes 8126464 | tf_op jit(solution)/shard_map/dot_general | solution.py:15
  (4 shorter events, 0.0 us)
Async XLA Ops:
  6.5 100.6 %all-to-all-start = ((bf16[8,128,2048]{2,1,0:T(8,128)(2,1)}), bf16[8,128,2048]{2,1,0:T(8,128)(2,1)}, u32[]{:S(2)}, u32[]{:S(2)}) async-start(bf16[8,128,2048]{2,1,0:T(8,128)(2,1)} %bitcast.24), calls=%async_computation | async-start | bytes 8388608 | tf_op jit(solution)/shard_map/all_to_all | solution.py:61
  13.8 1.5 copy-start
  13.8 109.5 %all-gather.11.cloned.1.call-start = ((), (), s32[]{:S(2)}) async-start(), calls=%async_computation.4 | async-start | bytes 2359296 | tf_op jit(solution)/shard_map/all_gather | solution.py:35
  14.6 205.3 %all-gather.13.cloned.1.call-start = ((), (), s32[]{:S(2)}) async-start(), calls=%async_computation.5 | async-start | bytes 12582912 | tf_op jit(solution)/shard_map/all_gather | solution.py:23
  116.6 4.8 %copy-start.1 = (s32[8]{0:T(128)S(1)}, s32[8]{0:T(128)}, u32[]{:S(2)}) copy-start(s32[8]{0:T(128)} %param.9) | copy-start | bytes 100
  116.6 97.2 %all-to-all-start.1 = ((bf16[8,128,2048]{2,1,0:T(8,128)(2,1)}), bf16[8,128,2048]{2,1,0:T(8,128)(2,1)}, u32[]{:S(2)}, u32[]{:S(2)}) async-start(bf16[8,128,2048]{2,1,0:T(8,128)(2,1)} %broadcast_select_fusion), calls=%async_computation.1 | async-start | bytes 8388608 | tf_op jit(solution)/shard_map/all_to_all | solution.py:62
  121.3 113.4 %all-gather.7.cloned.1.call-start = ((), (), s32[]{:S(2)}) async-start(), calls=%async_computation.2 | async-start | bytes 2359296 | tf_op jit(solution)/shard_map/all_gather | solution.py:39
  219.8 31.0 %all-gather.9.cloned.1.call-start = ((), (), s32[]{:S(2)}) async-start(), calls=%async_computation.3 | async-start | bytes 2359296 | tf_op jit(solution)/shard_map/all_gather | solution.py:45
Sparse Core Ops, SparseCore 0:
  16.2 11.1 all-gather.10
  29.0 21.0 all-gather.12
  219.9 8.8 all-gather.6
  241.9 8.8 all-gather.8
where the time goes:
time: 264 us; the launch traced here: 263 us
  waiting for transfers between devices  193 us (73%)
  matrix products  33.6 us (13%)
  between operations  13.9 us (5%)
  starting transfers between devices  12.1 us (5%)
  local copies, waits for them, and re-layouts  5.53 us (2%)
  other arithmetic  5.38 us (2%)
    all_to_all x1, waiting for transfers between devices, per_device(): lax.all_to_all(inverse[0], 'wide', split_axis=0, concat_axis=0, tiled=True)  91.6 us
    all_to_all x1, waiting for transfers between devices, per_device(): lax.all_to_all(regroup(spread, sources, wide_size), 'wide', split_axis=0,...  90.5 us
    dot_general x3, matrix products, product_step(): return jnp.dot(matrix, shard_rows, preferred_element_type=jnp.float32)  18.8 us
    dot_general x1, matrix products, build_factor(): jnp.einsum('rh,rc->hc', columns, masked, preferred_element_type=jnp.float32)  14.8 us
    all_gather x1, waiting for transfers between devices, correction_product(): lax.all_gather(curvature, 'grad', axis=0, tiled=True)  9.01 us
    all_to_all x1, starting transfers between devices, per_device(): lax.all_to_all(inverse[0], 'wide', split_axis=0, concat_axis=0, tiled=True)  7.28 us
  transfers between devices with their start and end apart: 6, of which 3 were waited for; matrix products, arithmetic and copies ran while one was open for 12% of the time, Pallas kernels for 0%

commit v1 on v0

--- a/solution.py
+++ b/solution.py
@@ -53,15 +53,79 @@
     return (2.0 * first_sum - correction).astype(jnp.bfloat16)
 
 
+def pack(rows):
+    core = lax.axis_index("grad")
+    half = rows.shape[0]
+    step = half // 8
+    square = lax.dynamic_slice_in_dim(rows, core * half, half, 1)
+    other = lax.dynamic_slice_in_dim(rows, (1 - core) * half, half, 1)
+    folded = []
+    for i in range(4):
+        j = 7 - i
+        folded.append(square[i * step : (i + 1) * step, i * step :])
+        folded.append(square[j * step : (j + 1) * step, j * step :])
+    flat = [piece.reshape(piece.shape[0], -1, 128).swapaxes(0, 1).reshape(-1, 128) for piece in folded]
+    quarter = half // 2
+    for h in range(2):
+        block = lax.dynamic_slice_in_dim(
+            other[h * quarter : (h + 1) * quarter], (h ^ core) * quarter, quarter, 1
+        )
+        flat.append(block.reshape(quarter, -1, 128).swapaxes(0, 1).reshape(-1, 128))
+    return jnp.concatenate(flat, axis=0)
+
+
+def unpack(flat, half):
+    core = lax.axis_index("grad")
+    step = half // 8
+    quarter = half // 2
+    at = 0
+
+    def take(height, width):
+        nonlocal at
+        count = height * width // 128
+        piece = flat[at : at + count]
+        at += count
+        return piece.reshape(width // 128, height, 128).swapaxes(0, 1).reshape(height, width)
+
+    strips = [None] * 8
+    for i in range(4):
+        for k in (i, 7 - i):
+            strips[k] = jnp.pad(take(step, half - k * step), ((0, 0), (k * step, 0)))
+    upper = jnp.concatenate(strips, axis=0)
+    block = jnp.arange(half, dtype=jnp.int32) // step
+    square = jnp.where(block[:, None] <= block[None, :], upper, upper.T)
+    own = [take(quarter, quarter) for _ in range(2)]
+    size = lax.axis_size("grad")
+    came = lax.ppermute(jnp.stack(own), "grad", [(c, (c + 1) % size) for c in range(size)])
+    turned = [came[0].T, came[1].T]
+    first = core == 0
+    missing = [jnp.where(first, turned[1], turned[0]), jnp.where(first, turned[0], turned[1])]
+    rows = []
+    for h in range(2):
+        left_own = first if h == 0 else jnp.logical_not(first)
+        left = jnp.where(left_own, own[h], missing[h])
+        right = jnp.where(left_own, missing[h], own[h])
+        rows.append(jnp.concatenate([left, right], axis=1))
+    other = jnp.concatenate(rows, axis=0)
+    return jnp.concatenate(
+        [jnp.where(first, square, other), jnp.where(first, other, square)], axis=1
+    )
+
+
 def per_device(activations, inverse, gradients, matching, live_rows):
     wide_size = lax.axis_size("wide")
     position = lax.axis_index("wide")
     places = jnp.arange(wide_size, dtype=jnp.int32)
     sources = jnp.sum(jnp.where(matching[None, :] == places[:, None], places[None, :], 0), axis=1)
-    spread = lax.all_to_all(inverse[0], "wide", split_axis=0, concat_axis=0, tiled=True)
-    settled = lax.all_to_all(
+    packed = pack(inverse[0])
+    count = packed.shape[0]
+    full = -(-count // (16 * wide_size)) * 16 * wide_size
+    packed = jnp.pad(packed, ((0, full - count), (0, 0)))
+    spread = lax.all_to_all(packed, "wide", split_axis=0, concat_axis=0, tiled=True)
+    moved = lax.all_to_all(
         regroup(spread, sources, wide_size), "wide", split_axis=0, concat_axis=0, tiled=True
     )
+    settled = unpack(moved, inverse.shape[1])
     result = precondition(settled, activations[0], gradients[0], live_rows[position])
     return result[None]
 

time: 264 us -> 218 us (0.83)
  waiting for transfers between devices: 193 us -> 109 us
  local copies, waits for them, and re-layouts: 5.53 us -> 31.4 us
  other arithmetic: 5.38 us -> 17.3 us
    all_to_all x1, waiting for transfers between devices: 91.6 us -> 49.4 us  [per_device(): lax.all_to_all(packed, 'wide', split_axis=0, concat_axis=0, tiled=True)]
    all_to_all x1, waiting for transfers between devices: 90.5 us -> 49.1 us  [per_device(): lax.all_to_all(regroup(spread, sources, wide_size), 'wide', split_axis=0,...]
    select_n x0 -> x3, other arithmetic: none -> 12.1 us  [the longest x1 10.6 us: unpack(): jnp.where(first, square, other)]
    unnamed x4 -> x41, local copies, waits for them, and re-layouts: 0.01 us -> 8.37 us
    slice x0 -> x18, local copies, waits for them, and re-layouts: none -> 8.09 us  [the longest x4 3.79 us: pack(): folded.append(square[i * step:(i + 1) * step, i * step:])]
    reshape x0 -> x9, local copies, waits for them, and re-layouts: none -> 3.86 us  [the longest x7 3.59 us: take(): piece.reshape(width // 128, height, 128).swapaxes(0, 1)]
    dynamic_slice x0 -> x2, local copies, waits for them, and re-layouts: none -> 3.04 us  [the longest x1 1.76 us: pack(): square = lax.dynamic_slice_in_dim(rows, core * half, half, 1)]
    concatenate x0 -> x3, local copies, waits for them, and re-layouts: none -> 2.78 us  [the longest x2 2.71 us: unpack(): upper = jnp.concatenate(strips, axis=0)]
  transfers between devices with their start and end apart: 6 -> 7, of which waited for: 3 -> 3; matrix products, arithmetic and copies ran while one was open for 12% -> 24% of each run, Pallas kernels for 0% -> 0%
where the time goes in v1:
time: 218 us
  waiting for transfers between devices  109 us (50%)
  matrix products  34.1 us (16%)
  local copies, waits for them, and re-layouts  31.4 us (14%)
  other arithmetic  17.3 us (8%)
  between operations  14.3 us (7%)
  starting transfers between devices  11.6 us (5%)
    all_to_all x1, waiting for transfers between devices, per_device(): lax.all_to_all(packed, 'wide', split_axis=0, concat_axis=0, tiled=True)  49.4 us
    all_to_all x1, waiting for transfers between devices, per_device(): lax.all_to_all(regroup(spread, sources, wide_size), 'wide', split_axis=0,...  49.1 us
    dot_general x3, matrix products, product_step(): return jnp.dot(matrix, shard_rows, preferred_element_type=jnp.float32)  19.3 us
    dot_general x1, matrix products, build_factor(): jnp.einsum('rh,rc->hc', columns, masked, preferred_element_type=jnp.float32)  14.8 us
    select_n x1, other arithmetic, unpack(): jnp.where(first, square, other)  10.6 us
    all_gather x1, waiting for transfers between devices, correction_product(): lax.all_gather(curvature, 'grad', axis=0, tiled=True)  9.08 us
    unnamed x41, local copies, waits for them, and re-layouts  8.37 us
    all_to_all x1, starting transfers between devices, per_device(): lax.all_to_all(packed, 'wide', split_axis=0, concat_axis=0, tiled=True)  7.28 us
  transfers between devices with their start and end apart: 7, of which 3 were waited for; matrix products, arithmetic and copies ran while one was open for 24% of the time, Pallas kernels for 0%

profile of v1, /device:TPU:0, one launch (start us, length us, event | category | flops | bytes accessed | tf_op | source)
XLA Modules:
  0.0 217.7 jit_solution(18335497123581765071)
XLA Ops:
  6.5 1.8 constant_dynamic-slice_fusion.2
  8.3 2.6 %copy.94 = bf16[1,1024,1024]{1,2,0:T(8,128)(2,1)} copy(bf16[1,1024,1024]{2,1,0:T(8,128)(2,1)S(1)} %constant_dynamic-slice_fusion.2) | data formatting | bytes 4194304
  10.9 0.8 slice.94
  11.6 0.8 slice.96
  12.5 0.9 slice.98
  13.4 0.9 slice.100
  14.3 0.9 slice.99
  15.2 0.9 slice.97
  16.2 1.0 slice.95
  17.1 1.0 slice.93
  18.1 1.3 constant_dynamic-slice_fusion
  19.4 0.2 copy.99
  19.6 0.3 copy.76
  19.9 0.2 copy.97
  20.1 0.3 copy.75
  20.4 0.1 copy.77
  20.5 0.1 copy.69
  20.6 0.1 copy.71
  20.8 0.1 copy.73
  20.9 0.2 copy.72
  21.1 0.2 copy.70
  21.3 0.2 copy.68
  21.5 0.2 copy.67
  22.0 1.4 copy-done.1
  23.5 7.3 %all-to-all-start = ((bf16[8,1088,128]{2,1,0:T(8,128)(2,1)}), bf16[8,1088,128]{2,1,0:T(8,128)(2,1)S(1)}, u32[]{:S(2)}, u32[]{:S(2)}) async-start(bf16[8,1088,128]{2,1,0:T(8,128)(2,1)} %bitcast.144), calls=%async_computation | async-start | bytes 4456448 | tf_op jit(solution)/shard_map/all_to_all | solution.py:124
  30.8 0.7 all-gather.11.cloned.1.call-update
  31.5 0.7 all-gather.13.cloned.1.call-update
  32.2 0.1 select_reduce_fusion
  32.4 49.4 %all-to-all-done = bf16[8,1088,128]{2,1,0:T(8,128)(2,1)S(1)} async-done(((bf16[8,1088,128]{2,1,0:T(8,128)(2,1)}), bf16[8,1088,128]{2,1,0:T(8,128)(2,1)S(1)}, u32[]{:S(2)}, u32[]{:S(2)}) %all-to-all-start) | async-done | bytes 2228256 | tf_op jit(solution)/shard_map/all_to_all | solution.py:124
  81.8 2.3 %gather_fusion = bf16[8,1088,128]{2,1,0:T(8,128)(2,1)} fusion(bf16[8,1088,128]{2,1,0:T(8,128)(2,1)S(1)} %all-to-all-done, s32[1024]{0:T(1024)S(1)} %pad_clamp_fusion), kind=kCustom, calls=%fused_computation | custom fusion | bytes 4456480 | tf_op jit(solution)/shard_map/jit(_take)/gather | solution.py:11
  84.0 3.3 %broadcast_select_fusion = bf16[8,1088,128]{2,1,0:T(8,128)(2,1)} fusion(bf16[8,1088,128]{2,1,0:T(8,128)(2,1)} %gather_fusion, pred[8]{0:T(512)(128)(4,1)S(1)} %compare_and_fusion), kind=kLoop, calls=%fused_computation.14 | loop fusion | flops 1114112 | bytes 4456456 | tf_op jit(solution)/shard_map/jit(_take)/select_n | solution.py:11
  87.4 3.8 %all-to-all-start.1 = ((bf16[8,1088,128]{2,1,0:T(8,128)(2,1)}), bf16[8,1088,128]{2,1,0:T(8,128)(2,1)S(1)}, u32[]{:S(2)}, u32[]{:S(2)}) async-start(bf16[8,1088,128]{2,1,0:T(8,128)(2,1)} %broadcast_select_fusion), calls=%async_computation.1 | async-start | bytes 4456448 | tf_op jit(solution)/shard_map/all_to_all | solution.py:125
  91.1 0.2 all-gather.7.cloned.1.call-start
  91.4 0.6 dynamic_slice.26
  92.6 0.7 iota_compare_fusion.1
  93.3 49.1 %all-to-all-done.1 = bf16[8,1088,128]{2,1,0:T(8,128)(2,1)S(1)} async-done(((bf16[8,1088,128]{2,1,0:T(8,128)(2,1)}), bf16[8,1088,128]{2,1,0:T(8,128)(2,1)S(1)}, u32[]{:S(2)}, u32[]{:S(2)}) %all-to-all-start.1) | async-done | bytes 2228256 | tf_op jit(solution)/shard_map/all_to_all | solution.py:125
  142.4 0.6 slice.108
  143.2 0.6 copy.113
  143.8 0.1 copy.86
  143.9 0.7 copy.87
  144.7 0.1 copy.85
  144.8 0.7 copy.112
  145.5 0.2 copy.83
  145.6 0.8 copy.84
  146.5 0.2 copy.81
  146.6 0.8 copy.82
  147.5 0.2 copy.79
  147.6 0.8 copy.80
  148.5 0.2 copy.78
  148.7 0.2 copy.92
  149.0 0.2 copy.91
  149.2 1.1 pad_maximum_fusion.7
  150.4 1.0 pad_dynamic-update-slice_fusion.6
  151.3 0.9 pad_dynamic-update-slice_fusion.5
  152.5 2.7 %copy.89 = bf16[1024,1024]{0,1:T(8,128)(2,1)} copy(bf16[1024,1024]{1,0:T(8,128)(2,1)S(1)} %pad_dynamic-update-slice_fusion) | data formatting | bytes 4194304 | tf_op jit(solution)/shard_map/concatenate | solution.py:94
  155.2 1.5 bitcast_select_fusion.5
  156.7 0.4 copy-done
  157.1 10.6 %broadcast_select_fusion.2 = (bf16[1024,1024]{1,0:T(8,128)(2,1)}, bf16[1024,1024]{1,0:T(8,128)(2,1)}) fusion(pred[]{:T(512)S(6)} %eq.14, bf16[512,512]{1,0:T(8,128)(2,1)S(1)} %get-tuple-element.15, bf16[512,512]{1,0:T(8,128)(2,1)S(1)} %get-tuple-element.16, bf16[512,512]{1,0:T(8,128)(2,1)S(1)} %get-tuple-element.12, ...), kind=kLoop, calls=%fused_computation.17 | loop fusion | flops 12582912 | bytes 10489857 | tf_op jit(solution)/shard_map/jit(_where)/select_n | solution.py:111
  167.7 6.4 %fusion.22 = (bf16[1024,384]{1,0:T(8,128)(2,1)}, f32[1024,384]{1,0:T(8,128)}) fusion(bf16[1,2048,384]{2,1,0:T(8,128)(2,1)} %all-gather.11.cloned.1.call-done, bf16[1024,1024]{1,0:T(8,128)(2,1)} %get-tuple-element.6, bf16[1024,1024]{1,0:T(8,128)(2,1)} %get-tuple-element.5), kind=kOutput, calls=%fused_computation.75 | convolution fusion | flops 1619394560 | bytes 8126464 | tf_op jit(solution)/shard_map/dot_general | solution.py:15
  174.1 0.3 all-gather.9.cloned.1.call-start
  174.4 14.8 %fusion = f32[1024,2048]{1,0:T(8,128)} fusion(bf16[1,2048,2048]{2,1,0:T(8,128)(2,1)} %all-gather.13.cloned.1.call-done, pred[2048]{0:T(1024)(128)(4,1)S(1)} %iota_compare_fusion.1, s32[]{:T(128)S(6)} %select_n.127), kind=kOutput, calls=%fused_computation.2 | convolution fusion | flops 8594128896 | bytes 20973572 | tf_op jit(solution)/shard_map/rh,rc->hc/dot_general | solution.py:27
  189.1 7.2 %fusion.9 = bf16[1024,384]{1,0:T(8,128)(2,1)} fusion(bf16[2048,384]{1,0:T(8,128)(2,1)} %all-gather.7.cloned.1.call-done, f32[1024,2048]{1,0:T(8,128)} %fusion, s32[1024]{0:T(1024)S(1)} %iota_add_fusion, f32[]{:T(128)S(6)} %convert_element_type.29), kind=kOutput, calls=%fused_computation.20 | convolution fusion | flops 1621491712 | bytes 10752004 | tf_op jit(solution)/shard_map/dot_general | solution.py:15
  196.4 9.1 %all-gather.9.cloned.1.call-done = bf16[2048,384]{1,0:T(8,128)(2,1)} async-done(((bf16[1024,384]{1,0:T(8,128)(2,1)}), bf16[2048,384]{1,0:T(8,128)(2,1)}) %all-gather.9.cloned.1.call-update) | async-done | bytes 1572880 | tf_op jit(solution)/shard_map/all_gather | solution.py:45
  205.5 5.7 %fusion.10 = bf16[1,1024,384]{2,1,0:T(8,128)(2,1)} fusion(bf16[2048,384]{1,0:T(8,128)(2,1)} %all-gather.9.cloned.1.call-done, bf16[1024,1024]{1,0:T(8,128)(2,1)} %get-tuple-element.6, bf16[1024,1024]{1,0:T(8,128)(2,1)S(1)} %copy-done.2, f32[1024,384]{1,0:T(8,128)} %get-tuple-element.18), kind=kOutput, calls=%fused_computation.21 | convolution fusion | flops 1620180992 | bytes 8126464 | tf_op jit(solution)/shard_map/dot_general | solution.py:15
  (57 shorter events, 0.9 us)
Async XLA Ops:
  22.0 1.4 copy-start.1
  23.5 58.3 %all-to-all-start = ((bf16[8,1088,128]{2,1,0:T(8,128)(2,1)}), bf16[8,1088,128]{2,1,0:T(8,128)(2,1)S(1)}, u32[]{:S(2)}, u32[]{:S(2)}) async-start(bf16[8,1088,128]{2,1,0:T(8,128)(2,1)} %bitcast.144), calls=%async_computation | async-start | bytes 4456448 | tf_op jit(solution)/shard_map/all_to_all | solution.py:124
  30.7 136.9 %all-gather.11.cloned.1.call-start = ((), (), s32[]{:S(2)}) async-start(), calls=%async_computation.4 | async-start | bytes 2359296 | tf_op jit(solution)/shard_map/all_gather | solution.py:35
  31.5 0.8 copy-start.8
  31.5 142.9 %all-gather.13.cloned.1.call-start = ((), (), s32[]{:S(2)}) async-start(), calls=%async_computation.5 | async-start | bytes 12582912 | tf_op jit(solution)/shard_map/all_gather | solution.py:23
  87.4 4.0 %copy-start.9 = (s32[8]{0:T(128)S(1)}, s32[8]{0:T(128)}, u32[]{:S(2)}) copy-start(s32[8]{0:T(128)} %param.9) | copy-start | bytes 100
  87.4 55.0 %all-to-all-start.1 = ((bf16[8,1088,128]{2,1,0:T(8,128)(2,1)}), bf16[8,1088,128]{2,1,0:T(8,128)(2,1)S(1)}, u32[]{:S(2)}, u32[]{:S(2)}) async-start(bf16[8,1088,128]{2,1,0:T(8,128)(2,1)} %broadcast_select_fusion), calls=%async_computation.1 | async-start | bytes 4456448 | tf_op jit(solution)/shard_map/all_to_all | solution.py:125
  91.1 98.0 %all-gather.7.cloned.1.call-start = ((), (), s32[]{:S(2)}) async-start(), calls=%async_computation.2 | async-start | bytes 2359296 | tf_op jit(solution)/shard_map/all_gather | solution.py:39
  149.2 3.1 %copy-start.3 = (bf16[128,640]{1,0:T(8,128)(2,1)S(1)}, bf16[128,640]{1,0:T(8,128)(2,1)}, u32[]{:S(2)}) copy-start(bf16[128,640]{1,0:T(8,128)(2,1)} %copy.84) | copy-start | bytes 491524
  149.2 3.2 %copy-start.4 = (bf16[16,8,4,128]{3,1,2,0:T(8,128)(2,1)S(1)}, bf16[16,8,4,128]{3,1,2,0:T(8,128)(2,1)}, u32[]{:S(2)}) copy-start(bf16[16,8,4,128]{3,1,2,0:T(8,128)(2,1)} %copy.112) | copy-start | bytes 393220
  149.2 3.2 %copy-start.5 = (bf16[128,384]{1,0:T(8,128)(2,1)S(1)}, bf16[128,384]{1,0:T(8,128)(2,1)}, u32[]{:S(2)}) copy-start(bf16[128,384]{1,0:T(8,128)(2,1)} %copy.87) | copy-start | bytes 294916
  149.2 3.2 %copy-start.6 = (bf16[16,8,2,128]{3,1,2,0:T(8,128)(2,1)S(1)}, bf16[16,8,2,128]{3,1,2,0:T(8,128)(2,1)}, u32[]{:S(2)}) copy-start(bf16[16,8,2,128]{3,1,2,0:T(8,128)(2,1)} %copy.113) | copy-start | bytes 196612
  149.2 3.2 %copy-start.7 = (bf16[128,128]{1,0:T(8,128)(2,1)S(1)}, bf16[128,128]{1,0:T(8,128)(2,1)}, u32[]{:S(2)}) copy-start(bf16[128,128]{1,0:T(8,128)(2,1)} %slice.108) | copy-start | bytes 98308
  150.3 4.8 %collective-permute-start = (bf16[2,512,512]{1,2,0:T(8,128)(2,1)}, bf16[2,512,512]{1,2,0:T(8,128)(2,1)}, u32[]{:S(2)}, u32[]{:S(2)}) collective-permute-start(bf16[2,512,512]{1,2,0:T(8,128)(2,1)} %pad_maximum_fusion.7), channel_id=1, source_target_pairs={{0,1},{1,0},{2,3},{3,2},{4,5},{5,4},{6,7},{7,6},{8,9},{9,8},{10,11... | collective-permute-start | bytes 3145736 | tf_op jit(solution)/shard_map/ppermute | solution.py:99
  155.2 1.9 copy-start
  174.1 31.4 %all-gather.9.cloned.1.call-start = ((), (), s32[]{:S(2)}) async-start(), calls=%async_computation.3 | async-start | bytes 2359296 | tf_op jit(solution)/shard_map/all_gather | solution.py:45
  189.1 16.3 %copy-start.2 = (bf16[1024,1024]{1,0:T(8,128)(2,1)S(1)}, bf16[1024,1024]{1,0:T(8,128)(2,1)}, u32[]{:S(2)}) copy-start(bf16[1024,1024]{1,0:T(8,128)(2,1)} %get-tuple-element.5) | copy-start | bytes 6291460
Sparse Core Ops, SparseCore 0:
  33.1 11.1 all-gather.10
  45.9 21.0 all-gather.12
  174.2 9.0 all-gather.6
  196.5 8.9 all-gather.8

commit v2 on v0

v2 whole, which is shorter than its diff:
```python
import functools

import jax
import jax.numpy as jnp
from jax import lax
from jax.experimental import pallas as pl
from jax.experimental.pallas import tpu as pltpu
from jax.sharding import PartitionSpec as P

DAMPING = 1.0
LANES = 128
CHUNKS = 4
MESH = pl.DeviceIdType.MESH


def dot(a, b):
    return jnp.dot(a, b, preferred_element_type=jnp.float32)


def kernel(
    n, half, cols, part,
    sources, live, act, inv, grad, out,
    packed, stage, moved, o_in, a_own, a_oth, lhs_t, m_own, m_oth,
    s_d, s_o, g_own, g_oth, first, acc, f_own, f_oth, c_own, c_oth,
    *rest,
):
    arrived = rest[:CHUNKS]
    (pack_sem, load_sem, send1, recv1, send2, recv2,
     send_a, recv_a, send_g, recv_g, send_o, recv_o, send_f, recv_f, send_c, recv_c) = rest[CHUNKS:]
    me = lax.axis_index("wide")
    core = lax.axis_index("grad")
    mate = 1 - core
    quarter = half // 2
    blocks = half // LANES
    o_rows = 2 * quarter * (quarter // LANES)

    def base(k):
        return o_rows + LANES * (k * (k + 1) // 2)

    barrier = pltpu.get_barrier_semaphore()

    copies = []
    for h in range(2):
        shift = jnp.where(core == h, 0, quarter)
        for b in range(quarter // LANES):
            source = pl.multiple_of(mate * half + shift + b * LANES, LANES)
            copies.append((
                inv.at[0, pl.ds(h * quarter, quarter), pl.ds(source, LANES)],
                packed.at[pl.ds(h * o_rows // 2 + b * quarter, quarter)],
            ))
    for k in range(blocks):
        source = pl.multiple_of(core * half + k * LANES, LANES)
        copies.append((
            inv.at[0, pl.ds(0, (k + 1) * LANES), pl.ds(source, LANES)],
            packed.at[pl.ds(base(k), (k + 1) * LANES)],
        ))
    copies = [pltpu.make_async_copy(s, d, pack_sem.at[i]) for i, (s, d) in enumerate(copies)]
    for c in copies:
        c.start()

    def greet(step, carry):
        pl.semaphore_signal(
            barrier, inc=1, device_id={"wide": lax.rem(me + step, n)}, device_id_type=MESH
        )
        return carry

    lax.fori_loop(1, n, greet, 0)
    pl.semaphore_signal(barrier, inc=1, device_id={"grad": mate}, device_id_type=MESH)
    pl.semaphore_wait(barrier, n)

    for c in copies:
        c.wait()

    for q in range(CHUNKS):
        def scatter(step, carry, q=q):
            peer = lax.rem(me + step, n)
            pltpu.make_async_remote_copy(
                src_ref=packed.at[pl.ds(pl.multiple_of((q * n + peer) * part, 16), part)],
                dst_ref=arrived[q].at[me],
                send_sem=send1.at[q],
                recv_sem=recv1.at[q],
                device_id={"wide": peer},
                device_id_type=MESH,
            ).start()
            return carry

        lax.fori_loop(1, n, scatter, 0)
        pltpu.make_async_copy(
            packed.at[pl.ds(pl.multiple_of((q * n + me) * part, 16), part)],
            arrived[q].at[me],
            recv1.at[q],
        ).start()

    def to_mate(src, dst, ssem, rsem):
        return pltpu.make_async_remote_copy(
            src_ref=src, dst_ref=dst, send_sem=ssem, recv_sem=rsem,
            device_id={"grad": mate}, device_id_type=MESH,
        )

    mine = pl.ds(pl.multiple_of(core * half, half), half)
    own_cols = pl.ds(pl.multiple_of(core * half, half), half)
    mate_cols = pl.ds(pl.multiple_of(mate * half, half), half)
    loads = [
        pltpu.make_async_copy(act.at[0, :, own_cols], a_own.at[mine], load_sem.at[0]),
        pltpu.make_async_copy(act.at[0, :, mate_cols], a_oth.at[mine], load_sem.at[1]),
        pltpu.make_async_copy(grad.at[0], g_own, load_sem.at[2]),
    ]
    swaps = [
        to_mate(act.at[0, :, mate_cols], a_own.at[mine], send_a.at[0], recv_a.at[0]),
        to_mate(act.at[0, :, own_cols], a_oth.at[mine], send_a.at[1], recv_a.at[1]),
        to_mate(grad.at[0], g_oth, send_g, recv_g),
    ]
    for c in loads + swaps:
        c.start()
    for c in loads:
        c.wait()
    for c in swaps:
        c.wait()

    count = live[me]
    width = lhs_t.shape[0]
    scale = count.astype(jnp.float32)

    def factor_rows(i, carry):
        strip = pl.ds(pl.multiple_of(i * width, width), width)
        keep = lax.broadcasted_iota(jnp.int32, (2 * half, width), 0) < count
        tile = a_own[:, strip]
        lhs_t[...] = jnp.where(keep, tile, jnp.zeros_like(tile)).T

        def factor_cols(j, inner):
            span = pl.ds(pl.multiple_of(j * width, width), width)
            row = i * width + lax.broadcasted_iota(jnp.int32, (width, width), 0)
            col = j * width + lax.broadcasted_iota(jnp.int32, (width, width), 1)
            m_own[strip, span] = (
                dot(lhs_t[...], a_own[:, span]) / scale + jnp.where(row == col, DAMPING, 0.0)
            ).astype(jnp.bfloat16)
            m_oth[strip, span] = (dot(lhs_t[...], a_oth[:, span]) / scale).astype(jnp.bfloat16)
            return inner

        return lax.fori_loop(0, half // width, factor_cols, carry)

    lax.fori_loop(0, half // width, factor_rows, 0)

    for q in range(CHUNKS):
        pltpu.make_async_copy(arrived[q], arrived[q], recv1.at[q]).wait()

        def choose(t, carry, q=q):
            stage[q * n + t] = arrived[q][sources[t]]
            return carry

        lax.fori_loop(0, n, choose, 0)
        landing = pl.ds(pl.multiple_of((q * n + me) * part, 16), part)

        def deliver(step, carry, q=q, landing=landing):
            peer = lax.rem(me + step, n)
            pltpu.make_async_remote_copy(
                src_ref=stage.at[q * n + peer],
                dst_ref=moved.at[landing],
                send_sem=send2.at[q],
                recv_sem=recv2.at[q],
                device_id={"wide": peer},
                device_id_type=MESH,
            ).start()
            return carry

        lax.fori_loop(1, n, deliver, 0)
        pltpu.make_async_copy(stage.at[q * n + me], moved.at[landing], recv2.at[q]).start()

    def off_product(h, left, x):
        shift = pl.multiple_of(jnp.where(core == h, 0, quarter), quarter)
        return dot(left[h, :, :quarter], x[pl.ds(shift, quarter)]) + dot(
            left[h, :, quarter:], x[pl.ds(pl.multiple_of(quarter - shift, quarter), quarter)]
        )

    off = to_mate(moved.at[pl.ds(0, o_rows)], o_in, send_o, recv_o)
    off_at, next_block = None, 0
    for q in range(CHUNKS):
        chunk = moved.at[pl.ds(q * n * part, n * part)]
        pltpu.make_async_copy(chunk, chunk, recv2.at[q]).wait()
        end = (q + 1) * n * part
        if off_at is None and end >= o_rows:
            off_at = q
            off.start()
            for h in range(2):
                for b in range(quarter // LANES):
                    s_o[h, :, b * LANES : (b + 1) * LANES] = moved[
                        pl.ds(h * o_rows // 2 + b * quarter, quarter)
                    ]
            off.wait()
            for h in range(2):
                other = jnp.where(mate == h, 0, o_rows // 2)
                for b in range(quarter // LANES):
                    at = pl.multiple_of(other + b * quarter, quarter)
                    s_o[h, b * LANES : (b + 1) * LANES, quarter:] = o_in[pl.ds(at, quarter)].T
            for h in range(2):
                first[h * quarter : (h + 1) * quarter] = off_product(h, s_o, g_oth)
        while off_at is not None and next_block < blocks and base(next_block + 1) <= end:
            k = next_block
            lanes = slice(k * LANES, (k + 1) * LANES)
            s_d[0 : (k + 1) * LANES, lanes] = moved[pl.ds(base(k), (k + 1) * LANES)]
            if k:
                s_d[lanes, 0 : k * LANES] = moved[pl.ds(base(k), k * LANES)].T
            next_block += 1

    tiles = [slice(i, i + width) for i in range(0, half, width)]
    for rows in tiles:
        first[rows] = first[rows] + dot(s_d[rows], g_own[...])
        f_own[rows] = first[rows].astype(jnp.bfloat16)
    swap = to_mate(f_own, f_oth, send_f, recv_f)
    swap.start()
    for rows in tiles:
        acc[rows] = dot(m_own[rows], f_own[...])
    swap.wait()
    for rows in tiles:
        c_own[rows] = (acc[rows] + dot(m_oth[rows], f_oth[...])).astype(jnp.bfloat16)
    swap = to_mate(c_own, c_oth, send_c, recv_c)
    swap.start()
    for rows in tiles:
        acc[rows] = 2.0 * first[rows] - dot(s_d[rows], c_own[...])
    swap.wait()
    for h in range(2):
        rows = slice(h * quarter, (h + 1) * quarter)
        out[0, rows] = (acc[rows] - off_product(h, s_o, c_oth)).astype(jnp.bfloat16)

    for q in range(CHUNKS):
        sent = moved.at[pl.ds(0, (n - 1) * part)]
        pltpu.make_async_copy(sent, sent, send1.at[q]).wait()
        pltpu.make_async_copy(sent, sent, send2.at[q]).wait()


def per_device(activations, inverse, gradients, matching, live_rows):
    n = lax.axis_size("wide")
    half, order = inverse.shape[1:]
    cols = gradients.shape[2]
    places = jnp.arange(n, dtype=jnp.int32)
    sources = jnp.sum(jnp.where(matching[None, :] == places[:, None], places[None, :], 0), axis=1)
    quarter = half // 2
    blocks = half // LANES
    o_rows = 2 * quarter * (quarter // LANES)
    used = o_rows + LANES * (blocks * (blocks + 1) // 2)
    part = -(-used // (16 * n * CHUNKS)) * 16
    full = part * n * CHUNKS
    bf16, f32 = jnp.bfloat16, jnp.float32
    dma = pltpu.SemaphoreType.DMA
    vmem = pltpu.VMEM
    pack_count = 2 * (quarter // LANES) + blocks
    scratch = [
        vmem((full, LANES), bf16),
        vmem((CHUNKS * n, part, LANES), bf16),
        vmem((full, LANES), bf16),
        vmem((o_rows, LANES), bf16),
        vmem((order, half), bf16),
        vmem((order, half), bf16),
        vmem((256, order), bf16),
        vmem((half, half), bf16),
        vmem((half, half), bf16),
        vmem((half, half), bf16),
        vmem((2, quarter, half), bf16),
        vmem((half, cols), bf16),
        vmem((half, cols), bf16),
        vmem((half, cols), f32),
        vmem((half, cols), f32),
        vmem((half, cols), bf16),
        vmem((half, cols), bf16),
        vmem((half, cols), bf16),
        vmem((half, cols), bf16),
    ]
    scratch += [vmem((n, part, LANES), bf16) for _ in range(CHUNKS)]
    scratch += [dma((pack_count,)), dma((3,))]
    scratch += [dma((CHUNKS,)) for _ in range(4)]
    scratch += [dma((2,)), dma((2,))] + [dma(()) for _ in range(8)]
    smem = pl.BlockSpec(memory_space=pltpu.SMEM)
    hbm = pl.BlockSpec(memory_space=pl.ANY)
    return pl.pallas_call(
        functools.partial(kernel, n, half, cols, part),
        out_shape=jax.ShapeDtypeStruct(gradients.shape, bf16),
        in_specs=[smem, smem, hbm, hbm, hbm],
        out_specs=pl.BlockSpec(memory_space=pltpu.VMEM),
        scratch_shapes=scratch,
        cost_estimate=pl.CostEstimate(
            flops=2 * half * order * (order + 3 * cols),
            bytes_accessed=4 * half * order + 4 * half * cols,
            transcendentals=0,
        ),
        compiler_params=pltpu.CompilerParams(
            collective_id=0, has_side_effects=True, vmem_limit_bytes=56 * 1024 * 1024
        ),
    )(sources, live_rows, activations, inverse, gradients)


def solution(mesh):
    return jax.shard_map(
        per_device,
        mesh=mesh,
        in_specs=(
            P(("dom", "wide"), "grad", None),
            P(("dom", "wide"), "grad", None),
            P(("dom", "wide"), "grad", None),
            P("dom"),
            P("dom"),
        ),
        out_specs=P(("dom", "wide"), "grad", None),
        check_vma=False,
    )
```

time: 264 us -> 114 us (0.43)
  waiting for transfers between devices: 193 us -> 0 us
  Pallas kernels: 0 us -> 109 us
  matrix products: 33.6 us -> 0 us
  between operations: 13.9 us -> 0.01 us
  starting transfers between devices: 12.1 us -> 0 us
  other arithmetic: 5.38 us -> 1.28 us
  local copies, waits for them, and re-layouts: 5.53 us -> 2.09 us
    all_to_all x2 -> x0, waiting for transfers between devices: 182 us -> none  [the longest x1 91.6 us: per_device(): lax.all_to_all(inverse[0], 'wide', split_axis=0, concat_axis=0, tiled=True)]
    pallas_call x0 -> x1, Pallas kernels: none -> 109 us  [per_device(): pl.pallas_call(functools.partial(kernel, n, half, cols, part), out_shape=...]
    dot_general x4 -> x0, matrix products: 33.6 us -> none  [the longest x3 18.8 us: product_step(): return jnp.dot(matrix, shard_rows, preferred_element_type=jnp.float32)]
    all_to_all x2 -> x0, starting transfers between devices: 12 us -> none  [the longest x1 7.28 us: per_device(): lax.all_to_all(inverse[0], 'wide', split_axis=0, concat_axis=0, tiled=True)]
    all_gather x4 -> x0, waiting for transfers between devices: 9.05 us -> none  [the longest x1 9.01 us: correction_product(): lax.all_gather(curvature, 'grad', axis=0, tiled=True)]
    gather x1 -> x0, local copies, waits for them, and re-layouts: 4.93 us -> none  [regroup(): return jnp.take(grouped, destination, axis=0).reshape(stacked.shape)]
    select_n x2 -> x0, other arithmetic: 4.59 us -> none  [regroup(): return jnp.take(grouped, destination, axis=0).reshape(stacked.shape)]
  transfers between devices with their start and end apart: 6 -> 0, of which waited for: 3 -> 0; matrix products, arithmetic and copies ran while one was open for 12% -> 0% of each run, Pallas kernels for 0% -> 0%
where the time goes in v2:
time: 114 us; the launch traced here: 113 us
  Pallas kernels  109 us (96%)
  local copies, waits for them, and re-layouts  2.09 us (2%)
  other arithmetic  1.28 us (1%)
    pallas_call x1, Pallas kernels, per_device(): pl.pallas_call(functools.partial(kernel, n, half, cols, part), out_shape=...  109 us

profile of v2, /device:TPU:0, one launch (start us, length us, event | category | flops | bytes accessed | tf_op | source)
XLA Modules:
  0.0 112.6 jit_solution(8749902484065108537)
XLA Ops:
  0.0 1.3 %select_reduce_fusion.sources = s32[8]{0:T(128)} fusion(s32[8]{0:T(128)} %param.8), kind=kLoop, calls=%fused_computation | loop fusion | flops 184 | bytes 64 | tf_op jit(solution)/shard_map/reduce_sum | solution.py:236
  1.3 109.2 %shard_map.55 = bf16[1,1024,384]{2,1,0:T(8,128)(2,1)} custom-call(s32[8]{0:T(128)} %select_reduce_fusion.sources, s32[8]{0:T(128)} %live.1, bf16[1,1024,2048]{2,1,0:T(8,128)(2,1)} %act.1, bf16[1,1024,2048]{2,1,0:T(8,128)(2,1)} %inv.1, bf16[1,1024,384]{2,1,0:T(8,128)(2,1)} %grad.1), custom_call_target="tpu_custom_call" | custom-call | flops 13421772800 | bytes 9961472 | tf_op jit(solution)/shard_map/pallas_call | solution.py:274
  110.5 2.1 %copy.7 = bf16[1,1024,384]{2,1,0:T(8,128)(2,1)} copy(bf16[1,1024,384]{2,1,0:T(8,128)(2,1)} %shard_map.55) | data formatting | bytes 1572864

commit v3 on v2

--- a/solution.py
+++ b/solution.py
@@ -9,7 +9,7 @@
 
 DAMPING = 1.0
 LANES = 128
-CHUNKS = 4
+CHUNKS = 8
 MESH = pl.DeviceIdType.MESH
 
 
@@ -18,15 +18,17 @@
 
 
 def kernel(
-    n, half, cols, part,
+    n, half, cols, parts,
     sources, live, act, inv, grad, out,
-    packed, stage, moved, o_in, a_own, a_oth, lhs_t, m_own, m_oth,
+    packed, moved, o_in, a_own, a_oth, lhs_t, m_own, m_oth,
     s_d, s_o, g_own, g_oth, first, acc, f_own, f_oth, c_own, c_oth,
     *rest,
 ):
-    arrived = rest[:CHUNKS]
+    chunks = len(parts)
+    starts = [n * sum(parts[:q]) for q in range(chunks + 1)]
+    arrived, stage = rest[:chunks], rest[chunks : 2 * chunks]
     (pack_sem, load_sem, send1, recv1, send2, recv2,
-     send_a, recv_a, send_g, recv_g, send_o, recv_o, send_f, recv_f, send_c, recv_c) = rest[CHUNKS:]
+     send_a, recv_a, send_g, recv_g, send_o, recv_o, send_f, recv_f, send_c, recv_c) = rest[2 * chunks :]
     me = lax.axis_index("wide")
     core = lax.axis_index("grad")
     mate = 1 - core
@@ -71,11 +73,11 @@
     for c in copies:
         c.wait()
 
-    for q in range(CHUNKS):
+    for q in range(chunks):
         def scatter(step, carry, q=q):
             peer = lax.rem(me + step, n)
             pltpu.make_async_remote_copy(
-                src_ref=packed.at[pl.ds(pl.multiple_of((q * n + peer) * part, 16), part)],
+                src_ref=packed.at[pl.ds(pl.multiple_of(starts[q] + peer * parts[q], 16), parts[q])],
                 dst_ref=arrived[q].at[me],
                 send_sem=send1.at[q],
                 recv_sem=recv1.at[q],
@@ -86,7 +88,7 @@
 
         lax.fori_loop(1, n, scatter, 0)
         pltpu.make_async_copy(
-            packed.at[pl.ds(pl.multiple_of((q * n + me) * part, 16), part)],
+            packed.at[pl.ds(pl.multiple_of(starts[q] + me * parts[q], 16), parts[q])],
             arrived[q].at[me],
             recv1.at[q],
         ).start()
@@ -141,20 +143,20 @@
 
     lax.fori_loop(0, half // width, factor_rows, 0)
 
-    for q in range(CHUNKS):
+    for q in range(chunks):
         pltpu.make_async_copy(arrived[q], arrived[q], recv1.at[q]).wait()
 
         def choose(t, carry, q=q):
-            stage[q * n + t] = arrived[q][sources[t]]
+            stage[q][t] = arrived[q][sources[t]]
             return carry
 
         lax.fori_loop(0, n, choose, 0)
-        landing = pl.ds(pl.multiple_of((q * n + me) * part, 16), part)
+        landing = pl.ds(pl.multiple_of(starts[q] + me * parts[q], 16), parts[q])
 
         def deliver(step, carry, q=q, landing=landing):
             peer = lax.rem(me + step, n)
             pltpu.make_async_remote_copy(
-                src_ref=stage.at[q * n + peer],
+                src_ref=stage[q].at[peer],
                 dst_ref=moved.at[landing],
                 send_sem=send2.at[q],
                 recv_sem=recv2.at[q],
@@ -164,7 +166,7 @@
             return carry
 
         lax.fori_loop(1, n, deliver, 0)
-        pltpu.make_async_copy(stage.at[q * n + me], moved.at[landing], recv2.at[q]).start()
+        pltpu.make_async_copy(stage[q].at[me], moved.at[landing], recv2.at[q]).start()
 
     def off_product(h, left, x):
         shift = pl.multiple_of(jnp.where(core == h, 0, quarter), quarter)
@@ -174,10 +176,10 @@
 
     off = to_mate(moved.at[pl.ds(0, o_rows)], o_in, send_o, recv_o)
     off_at, next_block = None, 0
-    for q in range(CHUNKS):
-        chunk = moved.at[pl.ds(q * n * part, n * part)]
+    for q in range(chunks):
+        chunk = moved.at[pl.ds(starts[q], n * parts[q])]
         pltpu.make_async_copy(chunk, chunk, recv2.at[q]).wait()
-        end = (q + 1) * n * part
+        end = starts[q + 1]
         if off_at is None and end >= o_rows:
             off_at = q
             off.start()
@@ -222,8 +224,8 @@
         rows = slice(h * quarter, (h + 1) * quarter)
         out[0, rows] = (acc[rows] - off_product(h, s_o, c_oth)).astype(jnp.bfloat16)
 
-    for q in range(CHUNKS):
-        sent = moved.at[pl.ds(0, (n - 1) * part)]
+    for q in range(chunks):
+        sent = moved.at[pl.ds(0, (n - 1) * parts[q])]
         pltpu.make_async_copy(sent, sent, send1.at[q]).wait()
         pltpu.make_async_copy(sent, sent, send2.at[q]).wait()
 
@@ -238,15 +240,16 @@
     blocks = half // LANES
     o_rows = 2 * quarter * (quarter // LANES)
     used = o_rows + LANES * (blocks * (blocks + 1) // 2)
-    part = -(-used // (16 * n * CHUNKS)) * 16
-    full = part * n * CHUNKS
+    units = -(-used // (16 * n))
+    per = -(-units // CHUNKS)
+    parts = [16 * min(per, units - at) for at in range(0, units, per)]
+    full = 16 * n * units
     bf16, f32 = jnp.bfloat16, jnp.float32
     dma = pltpu.SemaphoreType.DMA
     vmem = pltpu.VMEM
     pack_count = 2 * (quarter // LANES) + blocks
     scratch = [
         vmem((full, LANES), bf16),
-        vmem((CHUNKS * n, part, LANES), bf16),
         vmem((full, LANES), bf16),
         vmem((o_rows, LANES), bf16),
         vmem((order, half), bf16),
@@ -265,14 +268,14 @@
         vmem((half, cols), bf16),
         vmem((half, cols), bf16),
     ]
-    scratch += [vmem((n, part, LANES), bf16) for _ in range(CHUNKS)]
+    scratch += 2 * [vmem((n, part, LANES), bf16) for part in parts]
     scratch += [dma((pack_count,)), dma((3,))]
-    scratch += [dma((CHUNKS,)) for _ in range(4)]
+    scratch += [dma((len(parts),)) for _ in range(4)]
     scratch += [dma((2,)), dma((2,))] + [dma(()) for _ in range(8)]
     smem = pl.BlockSpec(memory_space=pltpu.SMEM)
     hbm = pl.BlockSpec(memory_space=pl.ANY)
     return pl.pallas_call(
-        functools.partial(kernel, n, half, cols, part),
+        functools.partial(kernel, n, half, cols, parts),
         out_shape=jax.ShapeDtypeStruct(gradients.shape, bf16),
         in_specs=[smem, smem, hbm, hbm, hbm],
         out_specs=pl.BlockSpec(memory_space=pltpu.VMEM),

time: 114 us -> 116 us (1.018)
  Pallas kernels: 109 us -> 112 us
    pallas_call x1, Pallas kernels: 109 us -> 112 us  [per_device(): pl.pallas_call(functools.partial(kernel, n, half, cols, parts), out_shape...]
where the time goes in v3:
time: 116 us
  Pallas kernels  112 us (97%)
  local copies, waits for them, and re-layouts  2.09 us (2%)
  other arithmetic  1.28 us (1%)
    pallas_call x1, Pallas kernels, per_device(): pl.pallas_call(functools.partial(kernel, n, half, cols, parts), out_shape...  112 us

profile of v3, /device:TPU:0, one launch (start us, length us, event | category | flops | bytes accessed | tf_op | source)
XLA Modules:
  0.0 115.6 jit_solution(6962491619160749124)
XLA Ops:
  0.0 1.3 %select_reduce_fusion.sources = s32[8]{0:T(128)} fusion(s32[8]{0:T(128)} %param.8), kind=kLoop, calls=%fused_computation | loop fusion | flops 184 | bytes 64 | tf_op jit(solution)/shard_map/reduce_sum | solution.py:238
  1.3 112.2 %shard_map.55 = bf16[1,1024,384]{2,1,0:T(8,128)(2,1)} custom-call(s32[8]{0:T(128)} %select_reduce_fusion.sources, s32[8]{0:T(128)} %live.1, bf16[1,1024,2048]{2,1,0:T(8,128)(2,1)} %act.1, bf16[1,1024,2048]{2,1,0:T(8,128)(2,1)} %inv.1, bf16[1,1024,384]{2,1,0:T(8,128)(2,1)} %grad.1), custom_call_target="tpu_custom_call" | custom-call | flops 13421772800 | bytes 9961472 | tf_op jit(solution)/shard_map/pallas_call | solution.py:277
  113.5 2.1 %copy.7 = bf16[1,1024,384]{2,1,0:T(8,128)(2,1)} copy(bf16[1,1024,384]{2,1,0:T(8,128)(2,1)} %shard_map.55) | data formatting | bytes 1572864

commit v4 on v2

--- a/solution.py
+++ b/solution.py
@@ -68,10 +68,14 @@
     pl.semaphore_signal(barrier, inc=1, device_id={"grad": mate}, device_id_type=MESH)
     pl.semaphore_wait(barrier, n)
 
-    for c in copies:
-        c.wait()
-
+    begins = [h * o_rows // 2 + b * quarter for h in range(2) for b in range(quarter // LANES)]
+    begins += [base(k) for k in range(blocks)]
+    waited = 0
     for q in range(CHUNKS):
+        while waited < len(copies) and (begins[waited] < (q + 1) * n * part or q == CHUNKS - 1):
+            copies[waited].wait()
+            waited += 1
+
         def scatter(step, carry, q=q):
             peer = lax.rem(me + step, n)
             pltpu.make_async_remote_copy(

time: 114 us -> 114 us (level)
  no operation moved by 1% of the time
where the time goes in v4:
time: 114 us; the launch traced here: 112 us
  Pallas kernels  109 us (96%)
  local copies, waits for them, and re-layouts  2.09 us (2%)
  other arithmetic  1.28 us (1%)
    pallas_call x1, Pallas kernels, per_device(): pl.pallas_call(functools.partial(kernel, n, half, cols, part), out_shape=...  109 us

profile of v4, /device:TPU:0, one launch (start us, length us, event | category | flops | bytes accessed | tf_op | source)
XLA Modules:
  0.0 112.2 jit_solution(4142561159027759528)
XLA Ops:
  0.0 1.3 %select_reduce_fusion.sources = s32[8]{0:T(128)} fusion(s32[8]{0:T(128)} %param.8), kind=kLoop, calls=%fused_computation | loop fusion | flops 184 | bytes 64 | tf_op jit(solution)/shard_map/reduce_sum | solution.py:240
  1.3 108.9 %shard_map.55 = bf16[1,1024,384]{2,1,0:T(8,128)(2,1)} custom-call(s32[8]{0:T(128)} %select_reduce_fusion.sources, s32[8]{0:T(128)} %live.1, bf16[1,1024,2048]{2,1,0:T(8,128)(2,1)} %act.1, bf16[1,1024,2048]{2,1,0:T(8,128)(2,1)} %inv.1, bf16[1,1024,384]{2,1,0:T(8,128)(2,1)} %grad.1), custom_call_target="tpu_custom_call" | custom-call | flops 13421772800 | bytes 9961472 | tf_op jit(solution)/shard_map/pallas_call | solution.py:278
  110.2 2.1 %copy.7 = bf16[1,1024,384]{2,1,0:T(8,128)(2,1)} copy(bf16[1,1024,384]{2,1,0:T(8,128)(2,1)} %shard_map.55) | data formatting | bytes 1572864
